TPU v7x, 32 devices: a whole 2x2x4 slice. The times are simulated.
32 devices in a mesh: groups: 2 (over y), seq: 8 (over z, x), section: 2 (over core).
Axes of the slice: x: 2, y: 2, z: 4, core: 2. Of those that a mesh axis runs over, the one named last changes fastest.
Arguments:
- skip_in: bfloat16 [2, 1024, 1536], P('groups', 'seq'), parts along dimension 0, may hold values from -6 to 6
- attn_gain: float32 [1536], replicated, may hold values from 0.25 to 1.75
- query_weight: bfloat16 [1536, 1024], P(None, 'section'), may hold values from -0.625 to 0.625
- kv_weight: bfloat16 [1536, 256], replicated, may hold values from -0.15625 to 0.15625
- pair_bias: float32 [2, 8, 32, 32], P('groups', 'section', 'seq'), parts along dimension 0, may hold values from -12 to 400
- out_weight: bfloat16 [1024, 1536], P('section'), may hold values from -0.1875 to 0.1875
- dec_gain: float32 [1536], replicated, may hold values from 0.25 to 1.75
- dec_weight: bfloat16 [5, 1536, 768], P(None, 'seq', 'section'), may hold values from -0.0625 to 0.0625
- dec_bias: float32 [768], P('section'), may hold values from -3 to 3
Outputs:
- decoded: bfloat16 [2, 1024, 768], P('groups', 'seq', 'section'), parts along dimension 0
There are 2 independent parts, one for each index of `groups`. A program takes and returns all parts, laid end to end along the dimension named above; an argument that names none is the same for every part. Nothing has to cross between parts.
All inputs are finite; a program needn't handle non-finite values.
Results may differ from a plain program's by a relative error of at most 0.0095.
Values may be sent and summed in bfloat16 or wider, within the bound.
A program may use at most 64 MiB of HBM per device.

v0:
```python
import math

import jax
import jax.numpy as jnp
from jax import lax
from jax.sharding import PartitionSpec as P

HEAD = 128
KW = 5
PAIR = 16


def extended(block, sides, width):
    for axis, dim in sides:
        count = lax.axis_size(axis)
        forward = [(i, i + 1) for i in range(count - 1)]
        backward = [(target, source) for source, target in forward]
        low = lax.ppermute(
            lax.slice_in_dim(block, block.shape[dim] - width, None, axis=dim), axis, forward
        )
        high = lax.ppermute(lax.slice_in_dim(block, 0, width, axis=dim), axis, backward)
        block = jnp.concatenate([low, block, high], axis=dim)
    return block


def norm_scale(values_in, gain):
    wide = values_in.astype(jnp.float32)
    return wide * lax.rsqrt(jnp.mean(wide * wide, axis=-1, keepdims=True) + 1e-06) * gain


def body(
    skip_in,
    attn_gain,
    query_weight,
    kv_weight,
    pair_bias,
    out_weight,
    dec_gain,
    dec_weight,
    dec_bias,
):
    seq_count, local_rows, channels = skip_in.shape
    half_rows = local_rows // 2
    local_heads = query_weight.shape[1] // HEAD
    logit_scale = 1.0 / math.sqrt(HEAD)
    pooled = jnp.max(skip_in.reshape(seq_count, half_rows, 2, channels), axis=2)
    normed = norm_scale(pooled, attn_gain).astype(jnp.bfloat16)
    flattened = normed.reshape(seq_count * half_rows, channels)
    query_rows = jnp.dot(flattened, query_weight, preferred_element_type=jnp.float32).astype(
        jnp.bfloat16
    )
    query_rows = query_rows.reshape(seq_count, half_rows, local_heads, HEAD)
    row_bias = jnp.repeat(pair_bias, PAIR, axis=2)
    row_bias = jnp.pad(row_bias, ((0, 0), (0, 0), (0, 0), (0, 2)))
    quarter = half_rows // 2
    own_rows = lax.dynamic_slice_in_dim(normed, lax.axis_index("section") * quarter, quarter, 1)
    key_values = jnp.dot(
        own_rows.reshape(seq_count * quarter, channels),
        kv_weight,
        preferred_element_type=jnp.float32,
    )
    key_values = key_values.astype(jnp.bfloat16).reshape(seq_count, quarter, 2 * HEAD)
    piece = lax.all_gather(key_values, ("seq", "section"), axis=1, tiled=True)
    start = jnp.int32(0)
    running_max = jnp.full((seq_count, local_heads, half_rows), -1e30, jnp.float32)
    running_sum = jnp.zeros((seq_count, local_heads, half_rows), jnp.float32)
    weighted = jnp.zeros((seq_count, local_heads, half_rows, HEAD), jnp.float32)
    piece_rows = piece.shape[1]
    block_size = min(piece_rows, 2048)
    for offset in range(0, piece_rows, block_size):
        piece_len = min(block_size, piece_rows - offset)
        sub_piece = piece[:, offset : offset + piece_len]
        key_portion = sub_piece[:, :, :HEAD]
        value_part = sub_piece[:, :, HEAD:]
        first_row = start + offset
        blocks = lax.dynamic_slice_in_dim(row_bias, first_row // PAIR, piece_len // PAIR + 2, 3)
        spread = jnp.repeat(blocks, PAIR, axis=3)
        key_bias = lax.dynamic_slice_in_dim(spread, first_row % PAIR, piece_len, 3)
        scores = (
            jnp.einsum(
                "wtzj,wgj->wztg", query_rows, key_portion, preferred_element_type=jnp.float32
            )
            * logit_scale
            + key_bias
        )
        new_max = jnp.maximum(running_max, jnp.max(scores, axis=-1))
        rescale = jnp.exp(running_max - new_max)
        exponent_scores = jnp.exp(scores - new_max[..., None])
        running_sum = running_sum * rescale + jnp.sum(exponent_scores, axis=-1)
        weighted = weighted * rescale[..., None] + jnp.einsum(
            "umrl,ult->umrt",
            exponent_scores.astype(jnp.bfloat16),
            value_part,
            preferred_element_type=jnp.float32,
        )
        running_max = new_max
    folded = (running_max, running_sum, weighted)
    running_max, running_sum, weighted = folded
    context = (weighted / running_sum[..., None]).astype(jnp.bfloat16)
    context = jnp.transpose(context, (0, 2, 1, 3)).reshape(
        seq_count * half_rows, local_heads * HEAD
    )
    partial_value = jnp.dot(context, out_weight, preferred_element_type=jnp.float32).reshape(
        seq_count, half_rows, channels
    )
    summed = lax.psum(partial_value.astype(jnp.bfloat16), "section").astype(jnp.float32)
    attended = (pooled.astype(jnp.float32) + summed).astype(jnp.bfloat16)
    joined = (
        jnp.repeat(attended, 2, axis=1).astype(jnp.float32) + skip_in.astype(jnp.float32)
    ).astype(jnp.bfloat16)
    activated = jax.nn.gelu(norm_scale(joined, dec_gain)).astype(jnp.bfloat16)
    padded = extended(activated, (("seq", 1),), KW // 2)
    out_half = dec_weight.shape[2]
    piece = lax.all_gather(dec_weight, "seq", axis=1, tiled=True)
    piece_rows = piece.shape[1]
    stacked = jnp.concatenate(
        [padded[:, tap_index : tap_index + local_rows] for tap_index in range(KW)], axis=2
    )
    stacked = stacked.reshape(seq_count * local_rows, KW * piece_rows)
    convolved = jnp.dot(
        stacked, piece.reshape(KW * piece_rows, out_half), preferred_element_type=jnp.float32
    )
    residual = lax.dynamic_slice_in_dim(joined, lax.axis_index("section") * out_half, out_half, 2)
    decoded = (
        convolved.reshape(seq_count, local_rows, out_half) + dec_bias + residual.astype(jnp.float32)
    )
    return decoded.astype(jnp.bfloat16)


def solution(mesh):
    return jax.shard_map(
        body,
        mesh=mesh,
        in_specs=(
            P("groups", "seq", None),
            P(),
            P(None, "section"),
            P(),
            P("groups", "section", "seq", None),
            P("section", None),
            P(),
            P(None, "seq", "section"),
            P("section"),
        ),
        out_specs=P("groups", "seq", "section"),
        check_vma=False,
    )
```

profile of v0, /device:TPU:0, one launch (start us, length us, event | category | flops | bytes accessed | tf_op | source)
XLA Modules:
  0.0 150.7 jit_solution(8483585687084230014)
XLA Ops:
  7.4 0.0 copy-start
  7.4 0.0 copy-start.2
  7.4 0.0 copy-start.1
  7.4 0.0 all-reduce.3.cloned.1.call-start
  7.4 2.0 %reshape.220 = bf16[64,2,1536]{2,1,0:T(2,128)(2,1)} reshape(bf16[1,128,1536]{2,1,0:T(8,128)(2,1)} %param.9) | data formatting | bytes 786432 | tf_op jit(solution)/shard_map/reshape | solution.py:46
  9.4 2.0 %reduce_max.18 = bf16[64,1536]{1,0:T(8,128)(2,1)S(1)} reduce(bf16[64,2,1536]{2,1,0:T(2,128)(2,1)} %reshape.220, bf16[]{:T(256)} %constant.24.clone.1), dimensions={1}, to_apply=%region_0.0 | reduce | flops 98304 | bytes 589826 | tf_op jit(solution)/shard_map/reduce_max | solution.py:46
  11.4 0.0 copy-start.4
  11.4 0.1 fusion.37
  11.5 0.8 convert_bitcast_fusion
  12.3 0.1 dynamic-slice.1
  12.4 0.0 copy-done.2
  12.4 1.5 %convolution_convert_fusion.2 = bf16[32,256]{1,0:T(8,128)(2,1)S(1)} fusion(bf16[1536,256]{1,0:T(8,128)(2,1)} %param.12, f32[1,64,1536]{2,1,0:T(8,128)} %convert_bitcast_fusion, s32[]{:T(128)S(6)} %select_n.15, f32[1536]{0:T(1024)S(1)} %copy-done.2, f32[32]{0:T(128)S(1)} %dynamic-slice.1), kind=kOutput, calls=%fused_computation.18 | convolution fusion | flops 25321472 | bytes 1005700 | tf_op jit(solution)/shard_map/dot_general | solution.py:57
  13.9 25.2 %all-gather = bf16[512,256]{1,0:T(8,128)(2,1)} all-gather(bf16[32,256]{1,0:T(8,128)(2,1)S(1)} %convolution_convert_fusion.2), channel_id=2, replica_groups=mesh['groups'=2,'seq'=8,'section'=2] {'seq','section'}, dimensions={0}, use_global_device_ids=true | all-gather | bytes 278528 | tf_op jit(solution)/shard_map/all_gather | solution.py:63
  39.1 0.0 copy-done.1
  39.1 0.4 fusion.19
  39.6 0.0 copy-done.4
  39.6 0.1 copy.16
  39.7 0.1 broadcast_in_dim.31
  39.8 0.1 slice.41
  39.9 0.3 copy.19
  40.2 1.2 fusion.63
  41.4 0.2 fusion.31
  41.7 1.2 fusion.20
  42.9 0.1 copy.18
  42.9 0.0 copy-done
  42.9 1.1 fusion
  44.0 0.0 all-reduce.3.cloned.1.call-update
  44.0 0.0 all-gather.3.cloned.1.call-start
  44.1 0.5 all-gather.3.cloned.1.call-update
  44.6 15.0 %all-reduce.3.cloned.1.call-done = bf16[1,64,1536]{2,1,0:T(8,128)(2,1)} async-done(((bf16[1,64,1536]{2,1,0:T(8,128)(2,1)}), bf16[1,64,1536]{2,1,0:T(8,128)(2,1)}) %all-reduce.3.cloned.1.call-update) | async-done | bytes 196624 | tf_op jit(solution)/shard_map/psum | solution.py:106
  59.6 1.0 fusion.46
  60.6 0.0 copy-start.3
  60.6 0.3 broadcast_in_dim.34
  60.9 0.5 convert_element_type.120
  61.4 1.2 fusion.21
  62.6 0.0 copy-done.3
  62.6 0.4 fusion.25
  63.0 3.6 %collective-permute-start = (bf16[1,2,1536]{2,1,0:T(2,128)(2,1)S(1)}, bf16[1,2,1536]{2,1,0:T(2,128)(2,1)S(1)}, u32[]{:S(2)}, u32[]{:S(2)}) collective-permute-start(bf16[1,2,1536]{2,1,0:T(2,128)(2,1)S(1)} %get-tuple-element.8), channel_id=1, source_target_pairs={{0,2},{2,4},{4,6},{6,8},{8,10},{10,12},{12,14},{1,3},{3,5},{5,7},{... | collective-permute-start | bytes 18440 | tf_op jit(solution)/shard_map/ppermute | solution.py:18
  66.7 0.0 copy-start.5
  66.7 1.3 collective-permute-start.1
  68.0 0.0 collective-permute-done
  68.0 0.8 fusion.36
  68.8 0.9 fusion.41
  69.7 1.2 constant_dynamic-update-slice_fusion
  70.9 1.3 collective-permute-done.1
  72.2 0.9 fusion.34
  73.1 0.9 fusion.40
  74.0 64.1 %all-gather.3.cloned.1.call-done = bf16[5,1536,384]{2,1,0:T(8,128)(2,1)} async-done(((bf16[5,192,384]{2,1,0:T(8,128)(2,1)}), bf16[5,1536,384]{2,1,0:T(8,128)(2,1)}) %all-gather.3.cloned.1.call-update) | async-done | bytes 5898256 | tf_op jit(solution)/shard_map/all_gather | solution.py:114
  138.1 0.0 copy-done.5
  138.1 5.1 %fusion.14 = bf16[1,128,384]{2,1,0:T(8,128)(2,1)} fusion(bf16[7680,384]{1,0:T(8,128)(2,1)} %bitcast.79, bf16[1,128,7680]{2,1,0:T(8,128)(2,1)} %fusion.40, bf16[1,128,1536]{2,1,0:T(8,128)(2,1)S(1)} %get-tuple-element.6, s32[]{:T(128)S(6)} %select_n.16, f32[384]{0:T(512)S(1)} %copy-done.5), kind=kOutput, calls=%fused_computation.11 | convolution fusion | flops 755171328 | bytes 8062468 | tf_op jit(solution)/shard_map/dot_general | solution.py:120
  (7 shorter events, 0.1 us)
Async XLA Ops:
  7.4 35.6 %copy-start = (bf16[512,1536]{1,0:T(8,128)(2,1)S(1)}, bf16[512,1536]{1,0:T(8,128)(2,1)}, u32[]{:S(2)}) copy-start(bf16[512,1536]{1,0:T(8,128)(2,1)} %param.14) | copy-start | bytes 4718596
  7.4 5.0 %copy-start.2 = (f32[1536]{0:T(1024)S(1)}, f32[1536]{0:T(1024)}, u32[]{:S(2)}) copy-start(f32[1536]{0:T(1024)} %param.10) | copy-start | bytes 18436
  7.4 31.7 %copy-start.1 = (bf16[1536,512]{1,0:T(8,128)(2,1)S(1)}, bf16[1536,512]{1,0:T(8,128)(2,1)}, u32[]{:S(2)}) copy-start(bf16[1536,512]{1,0:T(8,128)(2,1)} %param.11) | copy-start | bytes 4718596
  7.4 52.2 %all-reduce.3.cloned.1.call-start = ((), (), s32[]{:S(2)}) async-start(), calls=%async_computation | async-start | bytes 393216 | tf_op jit(solution)/shard_map/psum | solution.py:106
  11.4 28.2 %copy-start.4 = (f32[1,4,4,32]{3,2,1,0:T(4,128)S(1)}, f32[1,4,4,32]{3,2,1,0:T(4,128)}, u32[]{:S(2)}) copy-start(f32[1,4,4,32]{3,2,1,0:T(4,128)} %param.13) | copy-start | bytes 6148
  44.0 94.0 %all-gather.3.cloned.1.call-start = ((), (), s32[]{:S(2)}) async-start(), calls=%async_computation.1 | async-start | bytes 6635520 | tf_op jit(solution)/shard_map/all_gather | solution.py:114
  60.6 2.1 %copy-start.3 = (f32[1536]{0:T(1024)S(1)}, f32[1536]{0:T(1024)}, u32[]{:S(2)}) copy-start(f32[1536]{0:T(1024)} %param.15) | copy-start | bytes 18436
  63.0 5.0 %collective-permute-start = (bf16[1,2,1536]{2,1,0:T(2,128)(2,1)S(1)}, bf16[1,2,1536]{2,1,0:T(2,128)(2,1)S(1)}, u32[]{:S(2)}, u32[]{:S(2)}) collective-permute-start(bf16[1,2,1536]{2,1,0:T(2,128)(2,1)S(1)} %get-tuple-element.8), channel_id=1, source_target_pairs={{0,2},{2,4},{4,6},{6,8},{8,10},{10,12},{12,14},{1,3},{3,5},{5,7},{... | collective-permute-start | bytes 18440 | tf_op jit(solution)/shard_map/ppermute | solution.py:18
  66.7 71.4 %copy-start.5 = (f32[384]{0:T(512)S(1)}, f32[384]{0:T(512)}, u32[]{:S(2)}) copy-start(f32[384]{0:T(512)} %param.17) | copy-start | bytes 4612
  66.7 5.5 %collective-permute-start.1 = (bf16[1,2,1536]{2,1,0:T(2,128)(2,1)S(1)}, bf16[1,2,1536]{2,1,0:T(2,128)(2,1)S(1)}, u32[]{:S(2)}, u32[]{:S(2)}) collective-permute-start(bf16[1,2,1536]{2,1,0:T(2,128)(2,1)S(1)} %get-tuple-element.7), channel_id=1, source_target_pairs={{2,0},{4,2},{6,4},{8,6},{10,8},{12,10},{14,12},{3,1},{5,3},{7,5},{... | collective-permute-start | bytes 18440 | tf_op jit(solution)/shard_map/ppermute | solution.py:21
Sparse Core Ops, SparseCore 0:
  44.2 15.3 all-reduce.2
Sparse Core Ops, SparseCore 1:
  46.7 91.3 all-gather.2
where the time goes:
time: 151 us
  waiting for transfers between devices  81 us (54%)
  blocking collectives  25.2 us (17%)
  between operations  15 us (10%)
  matrix products  10.6 us (7%)
  other arithmetic  10.3 us (7%)
  starting transfers between devices  4.96 us (3%)
  local copies, waits for them, and re-layouts  3.61 us (2%)
    all_gather x1, waiting for transfers between devices, body(): piece = lax.all_gather(dec_weight, 'seq', axis=1, tiled=True)  64.1 us
    all_gather x1, blocking collectives, body(): piece = lax.all_gather(key_values, ('seq', 'section'), axis=1, tiled=True)  25.2 us
    psum x1, waiting for transfers between devices, body(): lax.psum(partial_value.astype(jnp.bfloat16), 'section').astype(jnp.float32)  15 us
    dot_general x1, matrix products, body(): jnp.dot(stacked, piece.reshape(KW * piece_rows, out_half), preferred_elem...  5.14 us
    unnamed x4, other arithmetic  3.74 us
    ppermute x1, starting transfers between devices, extended(): lax.ppermute(lax.slice_in_dim(block, block.shape[dim] - width, None, axis...  3.62 us
  transfers between devices with their start and end apart: 4, of which 3 were waited for; matrix products, arithmetic and copies ran while one was open for 5% of the time, Pallas kernels for 0%

commit v1 on v0

--- a/solution.py
+++ b/solution.py
@@ -1,8 +1,11 @@
+import functools
 import math
 
 import jax
 import jax.numpy as jnp
 from jax import lax
+from jax.experimental import pallas as pl
+from jax.experimental.pallas import tpu as pltpu
 from jax.sharding import PartitionSpec as P
 
 HEAD = 128
@@ -127,9 +130,465 @@
     return decoded.astype(jnp.bfloat16)
 
 
+def seq_pairs_fit(mesh, channels):
+    pairs = mesh.shape["seq"] // 2
+    return (
+        mesh.shape["groups"] == 2
+        and mesh.shape["section"] == 2
+        and mesh.shape["seq"] % 2 == 0
+        and pairs >= 2
+        and channels % (pairs * 128) == 0
+    )
+
+
+def dot(a, b):
+    return jnp.dot(a, b, preferred_element_type=jnp.float32)
+
+
+def select_matrix(rows, cols, chosen):
+    i = lax.broadcasted_iota(jnp.int32, (rows, cols), 0)
+    j = lax.broadcasted_iota(jnp.int32, (rows, cols), 1)
+    return jnp.where(chosen(i, j), 1.0, 0.0).astype(jnp.bfloat16)
+
+
+def block_kernel(
+    count,
+    skip_ref,
+    attn_gain_ref,
+    wq_hbm,
+    wkv_hbm,
+    bias_ref,
+    wout_hbm,
+    dec_gain_ref,
+    wdec_hbm,
+    dec_bias_ref,
+    out_ref,
+    wq,
+    wkv,
+    wout,
+    wdec,
+    pooled_ref,
+    kv,
+    spread,
+    partial,
+    part_out,
+    part_in,
+    act,
+    gathered,
+    edges,
+    padded,
+    resid,
+    resid_out,
+    conv_out,
+    conv_in,
+    local_sem,
+    kv_send,
+    kv_recv,
+    kvf_send,
+    kvf_recv,
+    w_send,
+    w_recv,
+    wf_send,
+    wf_recv,
+    sib_send,
+    sib_recv,
+    act_send,
+    act_recv,
+    actf_send,
+    actf_recv,
+    edge_send,
+    edge_recv,
+    conv_send,
+    conv_recv,
+):
+    g, s, k = lax.axis_index("groups"), lax.axis_index("seq"), lax.axis_index("section")
+    z, x = s // 2, s % 2
+    pairs = count // 2
+    local_rows, channels = skip_ref.shape
+    half = local_rows // 2
+    quarter = half // 2
+    heads = wq.shape[1] // HEAD
+    own_depth = wdec_hbm.shape[1]
+    mid_depth = own_depth // 2
+    out_half = wdec_hbm.shape[2]
+    width = channels // pairs
+    keys = kv.shape[0]
+    sibling = (g, s, 1 - k)
+
+    def remote(src, dst, send, recv, device):
+        return pltpu.make_async_remote_copy(
+            src_ref=src,
+            dst_ref=dst,
+            send_sem=send,
+            recv_sem=recv,
+            device_id=device,
+            device_id_type=pl.DeviceIdType.MESH,
+        )
+
+    def at(start, size, step):
+        return pl.ds(pl.multiple_of(start, step), size)
+
+    loads = [
+        pltpu.make_async_copy(wkv_hbm, wkv, local_sem.at[0]),
+        pltpu.make_async_copy(wq_hbm, wq, local_sem.at[1]),
+        pltpu.make_async_copy(wout_hbm, wout, local_sem.at[2]),
+        pltpu.make_async_copy(
+            wdec_hbm, wdec.at[:, at(x * own_depth, own_depth, 16)], local_sem.at[3]
+        ),
+    ]
+    for load in loads:
+        load.start()
+
+    barrier = pltpu.get_barrier_semaphore()
+    partners = [
+        (g, lax.rem(s + step, count), lax.rem(k + core, 2))
+        for step in range(count)
+        for core in range(2)
+        if step or core
+    ] + [(1 - g, s, k)]
+    for partner in partners:
+        pl.semaphore_signal(
+            barrier, inc=1, device_id=partner, device_id_type=pl.DeviceIdType.MESH
+        )
+
+    skip = skip_ref[...]
+    pooled = jnp.maximum(
+        dot(select_matrix(half, local_rows, lambda i, j: j == 2 * i), skip),
+        dot(select_matrix(half, local_rows, lambda i, j: j == 2 * i + 1), skip),
+    )
+    pooled_ref[...] = pooled
+    normed = norm_scale(pooled, attn_gain_ref[...]).astype(jnp.bfloat16)
+    loads[0].wait()
+    kv[at(s * half, half, 16), :] = dot(normed, wkv[...]).astype(jnp.bfloat16)
+
+    pl.semaphore_wait(barrier, len(partners))
+
+    def kv_rows(source, core):
+        return kv.at[at(source * half + core * quarter, quarter, 16)]
+
+    kv_copies = []
+    for step in range(1, count):
+        target = lax.rem(s + step, count)
+        copy = remote(
+            kv_rows(s, k), kv_rows(s, k), kv_send.at[step], kv_recv.at[step], (g, target, k)
+        )
+        copy.start()
+        kv_copies.append(copy)
+
+    pair = s + 1 - 2 * x
+    other_base = (1 - x) * own_depth
+    w_copies = []
+    for tap in range(KW):
+        copy = remote(
+            wdec_hbm.at[tap, at(g * mid_depth, mid_depth, 16)],
+            wdec.at[tap, at(x * own_depth + g * mid_depth, mid_depth, 16)],
+            w_send.at[tap],
+            w_recv.at[tap],
+            (g, pair, k),
+        )
+        copy.start()
+        w_copies.append(copy)
+    wf_copies = []
+
+    def pass_weight(tap):
+        w_copies[tap].wait_recv()
+        rows = wdec.at[tap, at(other_base + g * mid_depth, mid_depth, 16)]
+        copy = remote(rows, rows, wf_send.at[tap], wf_recv.at[tap], (1 - g, s, k))
+        copy.start()
+        wf_copies.append(copy)
+
+    loads[1].wait()
+    queries = dot(normed, wq[...]).astype(jnp.bfloat16)
+    queries = jnp.concatenate(
+        [queries[:, h * HEAD : (h + 1) * HEAD] for h in range(heads)], axis=0
+    )
+    cells = bias_ref.shape[2]
+    spreader = select_matrix(
+        cells, keys, lambda i, j: jnp.logical_and(j >= PAIR * i, j < PAIR * i + PAIR)
+    )
+    for h in range(heads):
+        rest = bias_ref[h]
+        total = None
+        for _ in range(3):
+            term = rest.astype(jnp.bfloat16)
+            rest = rest - term.astype(jnp.float32)
+            wide = dot(term, spreader)
+            total = wide if total is None else total + wide
+        for cell in range(half // PAIR):
+            spread[h * half + cell * PAIR : h * half + (cell + 1) * PAIR, :] = jnp.broadcast_to(
+                total[cell : cell + 1, :], (PAIR, keys)
+            )
+
+    kvf_copies = []
+    for step in range(1, count):
+        kv_copies[step - 1].wait_recv()
+        source = lax.rem(s - step + count, count)
+        copy = remote(
+            kv_rows(source, k),
+            kv_rows(source, k),
+            kvf_send.at[step],
+            kvf_recv.at[step],
+            sibling,
+        )
+        copy.start()
+        kvf_copies.append(copy)
+    for copy in kvf_copies:
+        copy.wait_recv()
+    for tap in range(3):
+        pass_weight(tap)
+
+    scores = lax.dot_general(
+        queries,
+        kv[:, :HEAD],
+        (((1,), (1,)), ((), ())),
+        preferred_element_type=jnp.float32,
+    ) * (1.0 / math.sqrt(HEAD)) + spread[...]
+    exponent = jnp.exp(scores - jnp.max(scores, axis=-1, keepdims=True))
+    totals = jnp.sum(exponent, axis=-1, keepdims=True)
+    context = (dot(exponent.astype(jnp.bfloat16), kv[:, HEAD:]) / totals).astype(jnp.bfloat16)
+    context = jnp.concatenate([context[h * half : (h + 1) * half] for h in range(heads)], axis=1)
+    loads[2].wait()
+    partial[...] = dot(context, wout[...])
+
+    part_out[...] = partial[at((1 - k) * quarter, quarter, 16), :].astype(jnp.bfloat16)
+    part_copy = remote(part_out, part_in, sib_send.at[0], sib_recv.at[0], sibling)
+    part_copy.start()
+    for tap in range(3, KW):
+        pass_weight(tap)
+    part_copy.wait_recv()
+    own = at(k * quarter, quarter, 16)
+    attended = (
+        pooled_ref[own, :] + (partial[own, :] + part_in[...].astype(jnp.float32))
+    ).astype(jnp.bfloat16)
+    repeater = select_matrix(
+        half, quarter, lambda i, j: jnp.logical_or(i == 2 * j, i == 2 * j + 1)
+    )
+    own_rows = at(k * half, half, 16)
+    joined = (dot(repeater, attended) + skip_ref[own_rows, :].astype(jnp.float32)).astype(
+        jnp.bfloat16
+    )
+    activated = jax.nn.gelu(norm_scale(joined, dec_gain_ref[...])).astype(jnp.bfloat16)
+    for chunk in range(pairs):
+        act[chunk] = activated[:, chunk * width : (chunk + 1) * width]
+
+    edge_copies = []
+    for step in range(pairs):
+        zz = lax.rem(z + step, pairs)
+        for core in range(2):
+            slot = step * 2 + core
+            copy = remote(
+                act.at[zz, at(k * (half - 16), 16, 16)],
+                edges.at[k, z],
+                edge_send.at[slot],
+                edge_recv.at[k, z],
+                (g, zz * 2 + 1 - x, core),
+            )
+            copy.start()
+            edge_copies.append(copy)
+    own_act = remote(
+        act.at[z], gathered.at[z, own_rows], sib_send.at[1], sib_recv.at[1], sibling
+    )
+    own_act.start()
+    act_copies = [None]
+    for step in range(1, pairs):
+        zz = lax.rem(z + step, pairs)
+        copy = remote(
+            act.at[zz],
+            gathered.at[z, own_rows],
+            act_send.at[step],
+            act_recv.at[step],
+            (g, zz * 2 + x, k),
+        )
+        copy.start()
+        act_copies.append(copy)
+    gathered[z, own_rows, :] = act[z]
+    for section in range(2):
+        resid_out[section] = joined[:, section * out_half : (section + 1) * out_half]
+    resid_copy = remote(
+        resid_out.at[1 - k], resid.at[own_rows], sib_send.at[2], sib_recv.at[2], sibling
+    )
+    resid_copy.start()
+    resid[own_rows, :] = resid_out[k]
+
+    actf_copies = [None]
+
+    def pass_act(step):
+        act_copies[step].wait_recv()
+        zz = lax.rem(z - step + pairs, pairs)
+        rows = gathered.at[zz, own_rows]
+        copy = remote(rows, rows, actf_send.at[step], actf_recv.at[step], sibling)
+        copy.start()
+        actf_copies.append(copy)
+
+    def convolve(zz):
+        low = jnp.maximum(zz - 1 + x, 0)
+        high = jnp.minimum(zz + x, pairs - 1)
+        low_edge = edges[1, low].astype(jnp.float32)
+        high_edge = edges[0, high].astype(jnp.float32)
+        padded[0:16, :] = jnp.where(zz - 1 + x >= 0, low_edge, 0.0)
+        padded[16 : 16 + local_rows, :] = gathered[zz].astype(jnp.float32)
+        padded[16 + local_rows : 32 + local_rows, :] = jnp.where(
+            zz + x < pairs, high_edge, 0.0
+        )
+        total = None
+        for tap in range(KW):
+            first = 16 + tap - KW // 2
+            window = padded[first : first + local_rows, :].astype(jnp.bfloat16)
+            term = dot(window, wdec[tap])
+            total = term if total is None else total + term
+        return total
+
+    loads[3].wait()
+    for copy in wf_copies:
+        copy.wait_recv()
+    own_act.wait_recv()
+    for core in range(2):
+        for zz in range(pairs):
+            remote(
+                act.at[0, pl.ds(0, 16)],
+                edges.at[core, zz],
+                edge_send.at[0],
+                edge_recv.at[core, zz],
+                sibling,
+            ).wait_recv()
+    pass_act(1)
+    result = convolve(z)
+    conv_copies = []
+    for step in range(1, pairs):
+        actf_copies[step].wait_recv()
+        if step + 1 < pairs:
+            pass_act(step + 1)
+        zz = lax.rem(z - step + pairs, pairs)
+        conv_out[step - 1] = convolve(zz).astype(jnp.bfloat16)
+        copy = remote(
+            conv_out.at[step - 1],
+            conv_in.at[step - 1],
+            conv_send.at[step],
+            conv_recv.at[step],
+            (g, zz * 2 + x, k),
+        )
+        copy.start()
+        conv_copies.append(copy)
+    resid_copy.wait_recv()
+    result = result + dec_bias_ref[...] + resid[...].astype(jnp.float32)
+    for step, copy in enumerate(conv_copies):
+        copy.wait_recv()
+        result = result + conv_in[step].astype(jnp.float32)
+    out_ref[...] = result.astype(jnp.bfloat16)
+    for copy in (
+        kv_copies
+        + kvf_copies
+        + w_copies
+        + wf_copies
+        + [part_copy, own_act, resid_copy]
+        + edge_copies
+        + act_copies[1:]
+        + actf_copies[1:]
+        + conv_copies
+    ):
+        copy.wait_send()
+
+
+def fused_body(
+    count,
+    skip_in,
+    attn_gain,
+    query_weight,
+    kv_weight,
+    pair_bias,
+    out_weight,
+    dec_gain,
+    dec_weight,
+    dec_bias,
+):
+    _, local_rows, channels = skip_in.shape
+    half = local_rows // 2
+    quarter = half // 2
+    pairs = count // 2
+    width = channels // pairs
+    heads = query_weight.shape[1] // HEAD
+    out_half = dec_weight.shape[2]
+    keys = half * count
+    bf16, f32 = jnp.bfloat16, jnp.float32
+    vmem = pl.BlockSpec(memory_space=pltpu.VMEM)
+    hbm = pl.BlockSpec(memory_space=pl.ANY)
+    dma = pltpu.SemaphoreType.DMA
+    scratch = [
+        pltpu.VMEM(query_weight.shape, bf16),
+        pltpu.VMEM(kv_weight.shape, bf16),
+        pltpu.VMEM(out_weight.shape, bf16),
+        pltpu.VMEM((KW, width, out_half), bf16),
+        pltpu.VMEM((half, channels), f32),
+        pltpu.VMEM((keys, 2 * HEAD), bf16),
+        pltpu.VMEM((heads * half, keys), f32),
+        pltpu.VMEM((half, channels), f32),
+        pltpu.VMEM((quarter, channels), bf16),
+        pltpu.VMEM((quarter, channels), bf16),
+        pltpu.VMEM((pairs, half, width), bf16),
+        pltpu.VMEM((pairs, local_rows, width), bf16),
+        pltpu.VMEM((2, pairs, 16, width), bf16),
+        pltpu.VMEM((local_rows + 32, width), f32),
+        pltpu.VMEM((local_rows, out_half), bf16),
+        pltpu.VMEM((2, half, out_half), bf16),
+        pltpu.VMEM((pairs - 1, local_rows, out_half), bf16),
+        pltpu.VMEM((pairs - 1, local_rows, out_half), bf16),
+        dma((4,)),
+        dma((count,)),
+        dma((count,)),
+        dma((count,)),
+        dma((count,)),
+        dma((KW,)),
+        dma((KW,)),
+        dma((KW,)),
+        dma((KW,)),
+        dma((3,)),
+        dma((3,)),
+        dma((pairs,)),
+        dma((pairs,)),
+        dma((pairs,)),
+        dma((pairs,)),
+        dma((2 * pairs,)),
+        dma((2, pairs)),
+        dma((pairs,)),
+        dma((pairs,)),
+    ]
+    decoded = pl.pallas_call(
+        functools.partial(block_kernel, count),
+        out_shape=jax.ShapeDtypeStruct((local_rows, out_half), bf16),
+        in_specs=[vmem, vmem, hbm, hbm, vmem, hbm, vmem, hbm, vmem],
+        out_specs=vmem,
+        scratch_shapes=scratch,
+        compiler_params=pltpu.CompilerParams(
+            collective_id=0, has_side_effects=True, vmem_limit_bytes=40 * 1024 * 1024
+        ),
+        cost_estimate=pl.CostEstimate(
+            flops=2 * local_rows * KW * channels * out_half,
+            bytes_accessed=6_000_000,
+            transcendentals=heads * half * keys,
+        ),
+    )(
+        skip_in[0],
+        attn_gain.reshape(1, channels),
+        query_weight,
+        kv_weight,
+        pair_bias[0],
+        out_weight,
+        dec_gain.reshape(1, channels),
+        dec_weight,
+        dec_bias.reshape(1, out_half),
+    )
+    return decoded[None]
+
+
 def solution(mesh):
+    def chosen(skip_in, *others):
+        fits = skip_in.shape[0] == 1 and skip_in.shape[1] % 64 == 0
+        if fits and seq_pairs_fit(mesh, skip_in.shape[2]):
+            return fused_body(mesh.shape["seq"], skip_in, *others)
+        return body(skip_in, *others)
+
     return jax.shard_map(
-        body,
+        chosen,
         mesh=mesh,
         in_specs=(
             P("groups", "seq", None),

time: 151 us -> 46.8 us (0.31)
  waiting for transfers between devices: 81 us -> 0 us
  Pallas kernels: 0 us -> 36.7 us
  blocking collectives: 25.2 us -> 0 us
  between operations: 15 us -> 0.02 us
  matrix products: 10.6 us -> 0 us
  other arithmetic: 10.3 us -> 0 us
  local copies, waits for them, and re-layouts: 3.61 us -> 9.48 us
  starting transfers between devices: 4.96 us -> 0 us
    all_gather x1 -> x0, waiting for transfers between devices: 64.1 us -> none  [body(): piece = lax.all_gather(dec_weight, 'seq', axis=1, tiled=True)]
    pallas_call x0 -> x1, Pallas kernels: none -> 36.7 us  [fused_body(): pl.pallas_call(functools.partial(block_kernel, count), out_shape=jax.Shap...]
    all_gather x1 -> x0, blocking collectives: 25.2 us -> none  [body(): piece = lax.all_gather(key_values, ('seq', 'section'), axis=1, tiled=True)]
    psum x1 -> x0, waiting for transfers between devices: 15 us -> none  [body(): lax.psum(partial_value.astype(jnp.bfloat16), 'section').astype(jnp.float32)]
    dot_general x6 -> x0, matrix products: 10.6 us -> none  [the longest x1 5.14 us: body(): jnp.dot(stacked, piece.reshape(KW * piece_rows, out_half), preferred_elem...]
    unnamed x13, local copies, waits for them, and re-layouts: 0.34 us -> 7.4 us
    ppermute x2 -> x0, starting transfers between devices: 4.92 us -> none  [the longest x1 3.62 us: extended(): lax.ppermute(lax.slice_in_dim(block, block.shape[dim] - width, None, axis...]
    unnamed x4 -> x0, other arithmetic: 3.74 us -> none
  transfers between devices with their start and end apart: 4 -> 0, of which waited for: 3 -> 0; matrix products, arithmetic and copies ran while one was open for 5% -> 0% of each run, Pallas kernels for 0% -> 0%
where the time goes in v1:
time: 46.8 us; the launch traced here: 46.2 us
  Pallas kernels  36.7 us (78%)
  local copies, waits for them, and re-layouts  9.48 us (20%)
    pallas_call x1, Pallas kernels, fused_body(): pl.pallas_call(functools.partial(block_kernel, count), out_shape=jax.Shap...  36.7 us
    unnamed x13, local copies, waits for them, and re-layouts  7.4 us

profile of v1, /device:TPU:0, one launch (start us, length us, event | category | flops | bytes accessed | tf_op | source)
XLA Modules:
  0.0 46.2 jit_solution(11873374909247365739)
XLA Ops:
  0.0 0.7 %reshape.11.dec_bias_ref = f32[1,384]{1,0:T(1,128)S(1)} reshape(f32[384]{0:T(512)} %param.17) | data formatting | bytes 3072 | tf_op jit(solution)/shard_map/reshape | solution.py:578
  0.7 0.7 %reshape.9.attn_gain_ref = f32[1,1536]{1,0:T(1,128)S(1)} reshape(f32[1536]{0:T(1024)} %param.10) | data formatting | bytes 12288 | tf_op jit(solution)/shard_map/reshape | solution.py:571
  1.4 0.7 %reshape.10.dec_gain_ref = f32[1,1536]{1,0:T(1,128)S(1)} reshape(f32[1536]{0:T(1024)} %param.15) | data formatting | bytes 12288 | tf_op jit(solution)/shard_map/reshape | solution.py:576
  2.1 0.0 copy-start
  2.1 1.4 %copy-done = bf16[1536,512]{1,0:T(8,128)(2,1)S(1)} copy-done((bf16[1536,512]{1,0:T(8,128)(2,1)S(1)}, bf16[1536,512]{1,0:T(8,128)(2,1)}, u32[]{:S(2)}) %copy-start) | copy-done | bytes 1572888
  3.5 0.0 copy-start.1
  3.5 1.4 %copy-done.1 = bf16[512,1536]{1,0:T(8,128)(2,1)S(1)} copy-done((bf16[512,1536]{1,0:T(8,128)(2,1)S(1)}, bf16[512,1536]{1,0:T(8,128)(2,1)}, u32[]{:S(2)}) %copy-start.1) | copy-done | bytes 1572888
  4.9 0.0 copy-start.2
  4.9 1.1 %copy-done.2 = bf16[1536,256]{1,0:T(8,128)(2,1)S(1)} copy-done((bf16[1536,256]{1,0:T(8,128)(2,1)S(1)}, bf16[1536,256]{1,0:T(8,128)(2,1)}, u32[]{:S(2)}) %copy-start.2) | copy-done | bytes 786456
  6.0 0.0 copy-start.3
  6.0 1.1 %copy-done.3 = bf16[5,192,384]{2,1,0:T(8,128)(2,1)S(1)} copy-done((bf16[5,192,384]{2,1,0:T(8,128)(2,1)S(1)}, bf16[5,192,384]{2,1,0:T(8,128)(2,1)}, u32[]{:S(2)}) %copy-start.3) | copy-done | bytes 737304
  7.2 0.0 copy-start.4
  7.2 1.0 %copy-done.4 = bf16[1,128,1536]{2,1,0:T(8,128)(2,1)S(1)} copy-done((bf16[1,128,1536]{2,1,0:T(8,128)(2,1)S(1)}, bf16[1,128,1536]{2,1,0:T(8,128)(2,1)}, u32[]{:S(2)}) %copy-start.4) | copy-done | bytes 393240
  8.2 0.0 copy-start.5
  8.2 0.7 %copy-done.5 = f32[1,4,4,32]{3,2,1,0:T(4,128)S(1)} copy-done((f32[1,4,4,32]{3,2,1,0:T(4,128)S(1)}, f32[1,4,4,32]{3,2,1,0:T(4,128)}, u32[]{:S(2)}) %copy-start.5) | copy-done | bytes 2072
  8.8 36.7 %shard_map.91 = bf16[128,384]{1,0:T(8,128)(2,1)S(1)} custom-call(bf16[128,1536]{1,0:T(8,128)(2,1)S(1)} %bitcast.3, f32[1,1536]{1,0:T(1,128)S(1)} %reshape.9.attn_gain_ref, bf16[1536,512]{1,0:T(8,128)(2,1)S(1)} %copy-done, bf16[1536,256]{1,0:T(8,128)(2,1)S(1)} %copy-done.2, f32[4,4,32]{2,1,0:T(4,128)S(1)} %bitcast.5, bf16[512,1536]{1,0:T(8,128)(2,1)S(1)} %copy-done.1, ...), custom_call_target="tpu_custom_call" | custom-call | flops 754974720 | bytes 6000000 | tf_op jit(solution)/shard_map/pallas_call | solution.py:555
  45.6 0.6 %copy.11 = bf16[1,128,384]{2,1,0:T(8,128)(2,1)} copy(bf16[1,128,384]{2,1,0:T(8,128)(2,1)S(1)} %bitcast.4) | data formatting | bytes 196608
Async XLA Ops:
  2.1 1.4 %copy-start = (bf16[1536,512]{1,0:T(8,128)(2,1)S(1)}, bf16[1536,512]{1,0:T(8,128)(2,1)}, u32[]{:S(2)}) copy-start(bf16[1536,512]{1,0:T(8,128)(2,1)} %wq_hbm.1) | copy-start | bytes 4718596
  3.5 1.4 %copy-start.1 = (bf16[512,1536]{1,0:T(8,128)(2,1)S(1)}, bf16[512,1536]{1,0:T(8,128)(2,1)}, u32[]{:S(2)}) copy-start(bf16[512,1536]{1,0:T(8,128)(2,1)} %wout_hbm.1) | copy-start | bytes 4718596
  4.9 1.1 %copy-start.2 = (bf16[1536,256]{1,0:T(8,128)(2,1)S(1)}, bf16[1536,256]{1,0:T(8,128)(2,1)}, u32[]{:S(2)}) copy-start(bf16[1536,256]{1,0:T(8,128)(2,1)} %wkv_hbm.1) | copy-start | bytes 2359300
  6.0 1.1 %copy-start.3 = (bf16[5,192,384]{2,1,0:T(8,128)(2,1)S(1)}, bf16[5,192,384]{2,1,0:T(8,128)(2,1)}, u32[]{:S(2)}) copy-start(bf16[5,192,384]{2,1,0:T(8,128)(2,1)} %wdec_hbm.1) | copy-start | bytes 2211844
  7.2 1.0 %copy-start.4 = (bf16[1,128,1536]{2,1,0:T(8,128)(2,1)S(1)}, bf16[1,128,1536]{2,1,0:T(8,128)(2,1)}, u32[]{:S(2)}) copy-start(bf16[1,128,1536]{2,1,0:T(8,128)(2,1)} %param.9) | copy-start | bytes 1179652
  8.2 0.7 %copy-start.5 = (f32[1,4,4,32]{3,2,1,0:T(4,128)S(1)}, f32[1,4,4,32]{3,2,1,0:T(4,128)}, u32[]{:S(2)}) copy-start(f32[1,4,4,32]{3,2,1,0:T(4,128)} %param.13) | copy-start | bytes 6148

commit v2 on v1

--- a/solution.py
+++ b/solution.py
@@ -153,16 +153,21 @@
 
 def block_kernel(
     count,
+    skip_hbm,
+    attn_gain_hbm,
+    wq_hbm,
+    wkv_hbm,
+    bias_hbm,
+    wout_hbm,
+    dec_gain_hbm,
+    wdec_hbm,
+    dec_bias_hbm,
+    out_ref,
     skip_ref,
     attn_gain_ref,
-    wq_hbm,
-    wkv_hbm,
     bias_ref,
-    wout_hbm,
     dec_gain_ref,
-    wdec_hbm,
     dec_bias_ref,
-    out_ref,
     wq,
     wkv,
     wout,
@@ -176,6 +181,7 @@
     act,
     gathered,
     edges,
+    outside,
     padded,
     resid,
     resid_out,
@@ -198,13 +204,15 @@
     actf_recv,
     edge_send,
     edge_recv,
+    outside_send,
+    outside_recv,
     conv_send,
     conv_recv,
 ):
     g, s, k = lax.axis_index("groups"), lax.axis_index("seq"), lax.axis_index("section")
-    z, x = s // 2, s % 2
     pairs = count // 2
-    local_rows, channels = skip_ref.shape
+    h, q = s // pairs, s % pairs
+    _, local_rows, channels = skip_hbm.shape
     half = local_rows // 2
     quarter = half // 2
     heads = wq.shape[1] // HEAD
@@ -228,13 +236,22 @@
     def at(start, size, step):
         return pl.ds(pl.multiple_of(start, step), size)
 
+    sources = [
+        (skip_hbm, skip_ref),
+        (attn_gain_hbm, attn_gain_ref),
+        (wkv_hbm, wkv),
+        (bias_hbm, bias_ref),
+        (wq_hbm, wq),
+        (wout_hbm, wout),
+        (dec_gain_hbm, dec_gain_ref),
+        (dec_bias_hbm, dec_bias_ref),
+    ] + [
+        (wdec_hbm.at[tap], wdec.at[at(tap * width + h * own_depth, own_depth, 16)])
+        for tap in range(KW)
+    ]
     loads = [
-        pltpu.make_async_copy(wkv_hbm, wkv, local_sem.at[0]),
-        pltpu.make_async_copy(wq_hbm, wq, local_sem.at[1]),
-        pltpu.make_async_copy(wout_hbm, wout, local_sem.at[2]),
-        pltpu.make_async_copy(
-            wdec_hbm, wdec.at[:, at(x * own_depth, own_depth, 16)], local_sem.at[3]
-        ),
+        pltpu.make_async_copy(src, dst, local_sem.at[slot])
+        for slot, (src, dst) in enumerate(sources)
     ]
     for load in loads:
         load.start()
@@ -251,14 +268,16 @@
             barrier, inc=1, device_id=partner, device_id_type=pl.DeviceIdType.MESH
         )
 
-    skip = skip_ref[...]
+    loads[0].wait()
+    skip = skip_ref[0]
     pooled = jnp.maximum(
         dot(select_matrix(half, local_rows, lambda i, j: j == 2 * i), skip),
         dot(select_matrix(half, local_rows, lambda i, j: j == 2 * i + 1), skip),
     )
     pooled_ref[...] = pooled
-    normed = norm_scale(pooled, attn_gain_ref[...]).astype(jnp.bfloat16)
-    loads[0].wait()
+    loads[1].wait()
+    normed = norm_scale(pooled, attn_gain_ref[...][None, :]).astype(jnp.bfloat16)
+    loads[2].wait()
     kv[at(s * half, half, 16), :] = dot(normed, wkv[...]).astype(jnp.bfloat16)
 
     pl.semaphore_wait(barrier, len(partners))
@@ -275,13 +294,13 @@
         copy.start()
         kv_copies.append(copy)
 
-    pair = s + 1 - 2 * x
-    other_base = (1 - x) * own_depth
+    pair = lax.rem(s + pairs, count)
+    other_base = (1 - h) * own_depth
     w_copies = []
     for tap in range(KW):
         copy = remote(
             wdec_hbm.at[tap, at(g * mid_depth, mid_depth, 16)],
-            wdec.at[tap, at(x * own_depth + g * mid_depth, mid_depth, 16)],
+            wdec.at[at(tap * width + h * own_depth + g * mid_depth, mid_depth, 16)],
             w_send.at[tap],
             w_recv.at[tap],
             (g, pair, k),
@@ -292,22 +311,23 @@
 
     def pass_weight(tap):
         w_copies[tap].wait_recv()
-        rows = wdec.at[tap, at(other_base + g * mid_depth, mid_depth, 16)]
+        rows = wdec.at[at(tap * width + other_base + g * mid_depth, mid_depth, 16)]
         copy = remote(rows, rows, wf_send.at[tap], wf_recv.at[tap], (1 - g, s, k))
         copy.start()
         wf_copies.append(copy)
 
-    loads[1].wait()
+    loads[4].wait()
     queries = dot(normed, wq[...]).astype(jnp.bfloat16)
     queries = jnp.concatenate(
-        [queries[:, h * HEAD : (h + 1) * HEAD] for h in range(heads)], axis=0
-    )
-    cells = bias_ref.shape[2]
+        [queries[:, i * HEAD : (i + 1) * HEAD] for i in range(heads)], axis=0
+    )
+    loads[3].wait()
+    cells = bias_ref.shape[3]
     spreader = select_matrix(
         cells, keys, lambda i, j: jnp.logical_and(j >= PAIR * i, j < PAIR * i + PAIR)
     )
-    for h in range(heads):
-        rest = bias_ref[h]
+    for head in range(heads):
+        rest = bias_ref[0, head]
         total = None
         for _ in range(3):
             term = rest.astype(jnp.bfloat16)
@@ -315,7 +335,8 @@
             wide = dot(term, spreader)
             total = wide if total is None else total + wide
         for cell in range(half // PAIR):
-            spread[h * half + cell * PAIR : h * half + (cell + 1) * PAIR, :] = jnp.broadcast_to(
+            first = head * half + cell * PAIR
+            spread[first : first + PAIR, :] = jnp.broadcast_to(
                 total[cell : cell + 1, :], (PAIR, keys)
             )
 
@@ -334,8 +355,7 @@
         kvf_copies.append(copy)
     for copy in kvf_copies:
         copy.wait_recv()
-    for tap in range(3):
-        pass_weight(tap)
+    pass_weight(0)
 
     scores = lax.dot_general(
         queries,
@@ -346,15 +366,14 @@
     exponent = jnp.exp(scores - jnp.max(scores, axis=-1, keepdims=True))
     totals = jnp.sum(exponent, axis=-1, keepdims=True)
     context = (dot(exponent.astype(jnp.bfloat16), kv[:, HEAD:]) / totals).astype(jnp.bfloat16)
-    context = jnp.concatenate([context[h * half : (h + 1) * half] for h in range(heads)], axis=1)
-    loads[2].wait()
+    context = jnp.concatenate([context[i * half : (i + 1) * half] for i in range(heads)], axis=1)
+    loads[5].wait()
     partial[...] = dot(context, wout[...])
 
     part_out[...] = partial[at((1 - k) * quarter, quarter, 16), :].astype(jnp.bfloat16)
     part_copy = remote(part_out, part_in, sib_send.at[0], sib_recv.at[0], sibling)
     part_copy.start()
-    for tap in range(3, KW):
-        pass_weight(tap)
+    pass_weight(1)
     part_copy.wait_recv()
     own = at(k * quarter, quarter, 16)
     attended = (
@@ -364,44 +383,75 @@
         half, quarter, lambda i, j: jnp.logical_or(i == 2 * j, i == 2 * j + 1)
     )
     own_rows = at(k * half, half, 16)
-    joined = (dot(repeater, attended) + skip_ref[own_rows, :].astype(jnp.float32)).astype(
+    joined = (dot(repeater, attended) + skip_ref[0, own_rows, :].astype(jnp.float32)).astype(
         jnp.bfloat16
     )
-    activated = jax.nn.gelu(norm_scale(joined, dec_gain_ref[...])).astype(jnp.bfloat16)
+    loads[6].wait()
+    activated = jax.nn.gelu(norm_scale(joined, dec_gain_ref[...][None, :])).astype(jnp.bfloat16)
     for chunk in range(pairs):
-        act[chunk] = activated[:, chunk * width : (chunk + 1) * width]
-
+        act[chunk] = jnp.concatenate(
+            [
+                activated[:, (chunk + i * pairs) * own_depth : (chunk + i * pairs + 1) * own_depth]
+                for i in range(2)
+            ],
+            axis=1,
+        )
+
+    edge_rows = at(k * (half - 16), 16, 16)
     edge_copies = []
     for step in range(pairs):
-        zz = lax.rem(z + step, pairs)
+        target = lax.rem(q + step, pairs)
         for core in range(2):
+            if step == 0 and core == 0:
+                continue
             slot = step * 2 + core
             copy = remote(
-                act.at[zz, at(k * (half - 16), 16, 16)],
-                edges.at[k, z],
+                act.at[target, edge_rows],
+                edges.at[k, q],
                 edge_send.at[slot],
-                edge_recv.at[k, z],
-                (g, zz * 2 + 1 - x, core),
+                edge_recv.at[k, q],
+                (g, h * pairs + target, lax.rem(k + core, 2)),
             )
             copy.start()
             edge_copies.append(copy)
+    edges[k, q] = act[q, edge_rows, :]
+    meets = jnp.logical_or(
+        jnp.logical_and(s == pairs - 1, k == 1), jnp.logical_and(s == pairs, k == 0)
+    )
+    outside_copies = [
+        remote(
+            act.at[target, edge_rows],
+            outside,
+            outside_send.at[target * 2 + core],
+            outside_recv.at[0],
+            (g, (1 - h) * pairs + target, core),
+        )
+        for target in range(pairs)
+        for core in range(2)
+    ]
+
+    @pl.when(meets)
+    def _():
+        for copy in outside_copies:
+            copy.start()
+
     own_act = remote(
-        act.at[z], gathered.at[z, own_rows], sib_send.at[1], sib_recv.at[1], sibling
+        act.at[q], gathered.at[q, own_rows], sib_send.at[1], sib_recv.at[1], sibling
     )
     own_act.start()
     act_copies = [None]
     for step in range(1, pairs):
-        zz = lax.rem(z + step, pairs)
+        target = lax.rem(q + step, pairs)
         copy = remote(
-            act.at[zz],
-            gathered.at[z, own_rows],
+            act.at[target],
+            gathered.at[q, own_rows],
             act_send.at[step],
             act_recv.at[step],
-            (g, zz * 2 + x, k),
+            (g, h * pairs + target, k),
         )
         copy.start()
         act_copies.append(copy)
-    gathered[z, own_rows, :] = act[z]
+    gathered[q, own_rows, :] = act[q]
     for section in range(2):
         resid_out[section] = joined[:, section * out_half : (section + 1) * out_half]
     resid_copy = remote(
@@ -414,63 +464,70 @@
 
     def pass_act(step):
         act_copies[step].wait_recv()
-        zz = lax.rem(z - step + pairs, pairs)
-        rows = gathered.at[zz, own_rows]
+        rows = gathered.at[lax.rem(q - step + pairs, pairs), own_rows]
         copy = remote(rows, rows, actf_send.at[step], actf_recv.at[step], sibling)
         copy.start()
         actf_copies.append(copy)
 
-    def convolve(zz):
-        low = jnp.maximum(zz - 1 + x, 0)
-        high = jnp.minimum(zz + x, pairs - 1)
-        low_edge = edges[1, low].astype(jnp.float32)
-        high_edge = edges[0, high].astype(jnp.float32)
-        padded[0:16, :] = jnp.where(zz - 1 + x >= 0, low_edge, 0.0)
-        padded[16 : 16 + local_rows, :] = gathered[zz].astype(jnp.float32)
+    def convolve(block):
+        outer = outside[...].astype(jnp.float32)
+        low = edges[1, jnp.maximum(block - 1, 0)].astype(jnp.float32)
+        low_outer = jnp.where(h == 1, outer, 0.0)
+        high = edges[0, jnp.minimum(block + 1, pairs - 1)].astype(jnp.float32)
+        high_outer = jnp.where(h == 0, outer, 0.0)
+        padded[0:16, :] = jnp.where(block == 0, low_outer, low)
+        padded[16 : 16 + local_rows, :] = gathered[block].astype(jnp.float32)
         padded[16 + local_rows : 32 + local_rows, :] = jnp.where(
-            zz + x < pairs, high_edge, 0.0
-        )
-        total = None
+            block == pairs - 1, high_outer, high
+        )
+        windows = []
         for tap in range(KW):
             first = 16 + tap - KW // 2
-            window = padded[first : first + local_rows, :].astype(jnp.bfloat16)
-            term = dot(window, wdec[tap])
-            total = term if total is None else total + term
-        return total
-
-    loads[3].wait()
+            windows.append(padded[first : first + local_rows, :].astype(jnp.bfloat16))
+        return dot(jnp.concatenate(windows, axis=1), wdec[...])
+
+    pass_weight(2)
+    pass_weight(3)
+    own_act.wait_recv()
+    for core in range(2):
+        for block in range(pairs):
+
+            @pl.when(jnp.logical_or(block != q, core != k))
+            def _():
+                remote(
+                    act.at[0, pl.ds(0, 16)],
+                    edges.at[core, block],
+                    edge_send.at[0],
+                    edge_recv.at[core, block],
+                    sibling,
+                ).wait_recv()
+
+    outside_copies[0].wait_recv()
+    pass_weight(4)
+    for load in loads[7:]:
+        load.wait()
     for copy in wf_copies:
         copy.wait_recv()
-    own_act.wait_recv()
-    for core in range(2):
-        for zz in range(pairs):
-            remote(
-                act.at[0, pl.ds(0, 16)],
-                edges.at[core, zz],
-                edge_send.at[0],
-                edge_recv.at[core, zz],
-                sibling,
-            ).wait_recv()
     pass_act(1)
-    result = convolve(z)
+    result = convolve(q)
     conv_copies = []
     for step in range(1, pairs):
         actf_copies[step].wait_recv()
         if step + 1 < pairs:
             pass_act(step + 1)
-        zz = lax.rem(z - step + pairs, pairs)
-        conv_out[step - 1] = convolve(zz).astype(jnp.bfloat16)
+        block = lax.rem(q - step + pairs, pairs)
+        conv_out[step - 1] = convolve(block).astype(jnp.bfloat16)
         copy = remote(
             conv_out.at[step - 1],
             conv_in.at[step - 1],
             conv_send.at[step],
             conv_recv.at[step],
-            (g, zz * 2 + x, k),
+            (g, h * pairs + block, k),
         )
         copy.start()
         conv_copies.append(copy)
     resid_copy.wait_recv()
-    result = result + dec_bias_ref[...] + resid[...].astype(jnp.float32)
+    result = result + dec_bias_ref[...][None, :] + resid[...].astype(jnp.float32)
     for step, copy in enumerate(conv_copies):
         copy.wait_recv()
         result = result + conv_in[step].astype(jnp.float32)
@@ -487,6 +544,11 @@
         + conv_copies
     ):
         copy.wait_send()
+
+    @pl.when(meets)
+    def _():
+        for copy in outside_copies:
+            copy.wait_send()
 
 
 def fused_body(
@@ -510,14 +572,18 @@
     out_half = dec_weight.shape[2]
     keys = half * count
     bf16, f32 = jnp.bfloat16, jnp.float32
-    vmem = pl.BlockSpec(memory_space=pltpu.VMEM)
-    hbm = pl.BlockSpec(memory_space=pl.ANY)
+    hbm = pl.BlockSpec(memory_space=pltpu.HBM)
     dma = pltpu.SemaphoreType.DMA
     scratch = [
+        pltpu.VMEM(skip_in.shape, bf16),
+        pltpu.VMEM(attn_gain.shape, f32),
+        pltpu.VMEM(pair_bias.shape, f32),
+        pltpu.VMEM(dec_gain.shape, f32),
+        pltpu.VMEM(dec_bias.shape, f32),
         pltpu.VMEM(query_weight.shape, bf16),
         pltpu.VMEM(kv_weight.shape, bf16),
         pltpu.VMEM(out_weight.shape, bf16),
-        pltpu.VMEM((KW, width, out_half), bf16),
+        pltpu.VMEM((KW * width, out_half), bf16),
         pltpu.VMEM((half, channels), f32),
         pltpu.VMEM((keys, 2 * HEAD), bf16),
         pltpu.VMEM((heads * half, keys), f32),
@@ -527,12 +593,13 @@
         pltpu.VMEM((pairs, half, width), bf16),
         pltpu.VMEM((pairs, local_rows, width), bf16),
         pltpu.VMEM((2, pairs, 16, width), bf16),
+        pltpu.VMEM((16, width), bf16),
         pltpu.VMEM((local_rows + 32, width), f32),
         pltpu.VMEM((local_rows, out_half), bf16),
         pltpu.VMEM((2, half, out_half), bf16),
         pltpu.VMEM((pairs - 1, local_rows, out_half), bf16),
         pltpu.VMEM((pairs - 1, local_rows, out_half), bf16),
-        dma((4,)),
+        dma((8 + KW,)),
         dma((count,)),
         dma((count,)),
         dma((count,)),
@@ -549,17 +616,19 @@
         dma((pairs,)),
         dma((2 * pairs,)),
         dma((2, pairs)),
+        dma((2 * pairs,)),
+        dma((1,)),
         dma((pairs,)),
         dma((pairs,)),
     ]
     decoded = pl.pallas_call(
         functools.partial(block_kernel, count),
         out_shape=jax.ShapeDtypeStruct((local_rows, out_half), bf16),
-        in_specs=[vmem, vmem, hbm, hbm, vmem, hbm, vmem, hbm, vmem],
-        out_specs=vmem,
+        in_specs=[hbm] * 9,
+        out_specs=pl.BlockSpec(memory_space=pltpu.VMEM),
         scratch_shapes=scratch,
         compiler_params=pltpu.CompilerParams(
-            collective_id=0, has_side_effects=True, vmem_limit_bytes=40 * 1024 * 1024
+            collective_id=0, has_side_effects=True, vmem_limit_bytes=63 * 1024 * 1024
         ),
         cost_estimate=pl.CostEstimate(
             flops=2 * local_rows * KW * channels * out_half,
@@ -567,15 +636,15 @@
             transcendentals=heads * half * keys,
         ),
     )(
-        skip_in[0],
-        attn_gain.reshape(1, channels),
+        skip_in,
+        attn_gain,
         query_weight,
         kv_weight,
-        pair_bias[0],
+        pair_bias,
         out_weight,
-        dec_gain.reshape(1, channels),
+        dec_gain,
         dec_weight,
-        dec_bias.reshape(1, out_half),
+        dec_bias,
     )
     return decoded[None]
 

time: 46.8 us -> 43.5 us (0.929)
  local copies, waits for them, and re-layouts: 9.48 us -> 1.54 us
  Pallas kernels: 36.7 us -> 41.8 us
    unnamed x13 -> x1, local copies, waits for them, and re-layouts: 7.4 us -> 1.54 us
    pallas_call x1, Pallas kernels: 36.7 us -> 41.8 us  [fused_body(): pl.pallas_call(functools.partial(block_kernel, count), out_shape=jax.Shap...]
    reshape x3 -> x0, local copies, waits for them, and re-layouts: 2.08 us -> none  [the longest x1 0.7 us: fused_body(): attn_gain.reshape(1, channels)]
where the time goes in v2:
time: 43.5 us; the launch traced here: 43.4 us
  Pallas kernels  41.8 us (96%)
  local copies, waits for them, and re-layouts  1.54 us (4%)
    pallas_call x1, Pallas kernels, fused_body(): pl.pallas_call(functools.partial(block_kernel, count), out_shape=jax.Shap...  41.8 us
    unnamed x1, local copies, waits for them, and re-layouts  1.54 us

profile of v2, /device:TPU:0, one launch (start us, length us, event | category | flops | bytes accessed | tf_op | source)
XLA Modules:
  0.0 43.4 jit_solution(5608917164524138847)
XLA Ops:
  0.0 41.8 %shard_map.91 = bf16[128,384]{1,0:T(8,128)(2,1)} custom-call(bf16[1,128,1536]{2,1,0:T(8,128)(2,1)} %skip_hbm.1, f32[1536]{0:T(1024)} %attn_gain_hbm.1, bf16[1536,512]{1,0:T(8,128)(2,1)} %wq_hbm.1, bf16[1536,256]{1,0:T(8,128)(2,1)} %wkv_hbm.1, f32[1,4,4,32]{3,2,1,0:T(4,128)} %bias_hbm.1, bf16[512,1536]{1,0:T(8,128)(2,1)} %wout_hbm.1, f32[1536]{0:T(1024)} %dec_gain_hbm.1, ...), custom_call_target="tpu_custom_call" | custom-call | flops 754974720 | bytes 6000000 | tf_op jit(solution)/shard_map/pallas_call | solution.py:624
  41.8 1.5 %copy.11 = bf16[1,128,384]{2,1,0:T(8,128)(2,1)} copy(bf16[1,128,384]{2,1,0:T(8,128)(2,1)} %bitcast.1) | data formatting | bytes 196608

commit v3 on v2

--- a/solution.py
+++ b/solution.py
@@ -137,6 +137,7 @@
         and mesh.shape["section"] == 2
         and mesh.shape["seq"] % 2 == 0
         and pairs >= 2
+        and pairs & (pairs - 1) == 0
         and channels % (pairs * 128) == 0
     )
 
@@ -181,7 +182,6 @@
     act,
     gathered,
     edges,
-    outside,
     padded,
     resid,
     resid_out,
@@ -204,14 +204,12 @@
     actf_recv,
     edge_send,
     edge_recv,
-    outside_send,
-    outside_recv,
     conv_send,
     conv_recv,
 ):
     g, s, k = lax.axis_index("groups"), lax.axis_index("seq"), lax.axis_index("section")
     pairs = count // 2
-    h, q = s // pairs, s % pairs
+    z, x = s // 2, s % 2
     _, local_rows, channels = skip_hbm.shape
     half = local_rows // 2
     quarter = half // 2
@@ -246,14 +244,14 @@
         (dec_gain_hbm, dec_gain_ref),
         (dec_bias_hbm, dec_bias_ref),
     ] + [
-        (wdec_hbm.at[tap], wdec.at[at(tap * width + h * own_depth, own_depth, 16)])
+        (wdec_hbm.at[tap], wdec.at[at(tap * width + x * own_depth, own_depth, 16)])
         for tap in range(KW)
     ]
     loads = [
         pltpu.make_async_copy(src, dst, local_sem.at[slot])
         for slot, (src, dst) in enumerate(sources)
     ]
-    for load in loads:
+    for load in loads[:3]:
         load.start()
 
     barrier = pltpu.get_barrier_semaphore()
@@ -269,6 +267,8 @@
         )
 
     loads[0].wait()
+    for load in loads[3:]:
+        load.start()
     skip = skip_ref[0]
     pooled = jnp.maximum(
         dot(select_matrix(half, local_rows, lambda i, j: j == 2 * i), skip),
@@ -294,13 +294,13 @@
         copy.start()
         kv_copies.append(copy)
 
-    pair = lax.rem(s + pairs, count)
-    other_base = (1 - h) * own_depth
+    pair = s + 1 - 2 * x
+    other_base = (1 - x) * own_depth
     w_copies = []
     for tap in range(KW):
         copy = remote(
             wdec_hbm.at[tap, at(g * mid_depth, mid_depth, 16)],
-            wdec.at[at(tap * width + h * own_depth + g * mid_depth, mid_depth, 16)],
+            wdec.at[at(tap * width + x * own_depth + g * mid_depth, mid_depth, 16)],
             w_send.at[tap],
             w_recv.at[tap],
             (g, pair, k),
@@ -356,6 +356,7 @@
     for copy in kvf_copies:
         copy.wait_recv()
     pass_weight(0)
+    pass_weight(1)
 
     scores = lax.dot_general(
         queries,
@@ -373,7 +374,8 @@
     part_out[...] = partial[at((1 - k) * quarter, quarter, 16), :].astype(jnp.bfloat16)
     part_copy = remote(part_out, part_in, sib_send.at[0], sib_recv.at[0], sibling)
     part_copy.start()
-    pass_weight(1)
+    pass_weight(2)
+    pass_weight(3)
     part_copy.wait_recv()
     own = at(k * quarter, quarter, 16)
     attended = (
@@ -389,69 +391,49 @@
     loads[6].wait()
     activated = jax.nn.gelu(norm_scale(joined, dec_gain_ref[...][None, :])).astype(jnp.bfloat16)
     for chunk in range(pairs):
-        act[chunk] = jnp.concatenate(
-            [
-                activated[:, (chunk + i * pairs) * own_depth : (chunk + i * pairs + 1) * own_depth]
-                for i in range(2)
-            ],
-            axis=1,
-        )
-
-    edge_rows = at(k * (half - 16), 16, 16)
+        act[chunk] = activated[:, chunk * width : (chunk + 1) * width]
+
+    masks = sorted(range(1, pairs), key=lambda mask: (mask < pairs // 2, mask))
+
+    def partner(mask):
+        result = z
+        bit = 1
+        while bit < pairs:
+            if mask & bit:
+                result = result + bit * (1 - 2 * ((z // bit) % 2))
+            bit *= 2
+        return result
+
     edge_copies = []
-    for step in range(pairs):
-        target = lax.rem(q + step, pairs)
+    for mask in masks + [0]:
+        target = partner(mask)
         for core in range(2):
-            if step == 0 and core == 0:
-                continue
-            slot = step * 2 + core
             copy = remote(
-                act.at[target, edge_rows],
-                edges.at[k, q],
-                edge_send.at[slot],
-                edge_recv.at[k, q],
-                (g, h * pairs + target, lax.rem(k + core, 2)),
+                act.at[target, at(k * (half - 16), 16, 16)],
+                edges.at[k, z],
+                edge_send.at[mask * 2 + core],
+                edge_recv.at[k, z],
+                (g, target * 2 + 1 - x, core),
             )
             copy.start()
             edge_copies.append(copy)
-    edges[k, q] = act[q, edge_rows, :]
-    meets = jnp.logical_or(
-        jnp.logical_and(s == pairs - 1, k == 1), jnp.logical_and(s == pairs, k == 0)
-    )
-    outside_copies = [
-        remote(
-            act.at[target, edge_rows],
-            outside,
-            outside_send.at[target * 2 + core],
-            outside_recv.at[0],
-            (g, (1 - h) * pairs + target, core),
-        )
-        for target in range(pairs)
-        for core in range(2)
-    ]
-
-    @pl.when(meets)
-    def _():
-        for copy in outside_copies:
-            copy.start()
-
     own_act = remote(
-        act.at[q], gathered.at[q, own_rows], sib_send.at[1], sib_recv.at[1], sibling
+        act.at[z], gathered.at[z, own_rows], sib_send.at[1], sib_recv.at[1], sibling
     )
     own_act.start()
-    act_copies = [None]
-    for step in range(1, pairs):
-        target = lax.rem(q + step, pairs)
+    act_copies = {}
+    for step in masks:
+        target = partner(step)
         copy = remote(
             act.at[target],
-            gathered.at[q, own_rows],
+            gathered.at[z, own_rows],
             act_send.at[step],
             act_recv.at[step],
-            (g, h * pairs + target, k),
+            (g, target * 2 + x, k),
         )
         copy.start()
-        act_copies.append(copy)
-    gathered[q, own_rows, :] = act[q]
+        act_copies[step] = copy
+    gathered[z, own_rows, :] = act[z]
     for section in range(2):
         resid_out[section] = joined[:, section * out_half : (section + 1) * out_half]
     resid_copy = remote(
@@ -460,69 +442,57 @@
     resid_copy.start()
     resid[own_rows, :] = resid_out[k]
 
-    actf_copies = [None]
+    actf_copies = {}
 
     def pass_act(step):
         act_copies[step].wait_recv()
-        rows = gathered.at[lax.rem(q - step + pairs, pairs), own_rows]
+        rows = gathered.at[partner(step), own_rows]
         copy = remote(rows, rows, actf_send.at[step], actf_recv.at[step], sibling)
         copy.start()
-        actf_copies.append(copy)
+        actf_copies[step] = copy
 
     def convolve(block):
-        outer = outside[...].astype(jnp.float32)
-        low = edges[1, jnp.maximum(block - 1, 0)].astype(jnp.float32)
-        low_outer = jnp.where(h == 1, outer, 0.0)
-        high = edges[0, jnp.minimum(block + 1, pairs - 1)].astype(jnp.float32)
-        high_outer = jnp.where(h == 0, outer, 0.0)
-        padded[0:16, :] = jnp.where(block == 0, low_outer, low)
+        low = edges[1, jnp.maximum(block - 1 + x, 0)].astype(jnp.float32)
+        high = edges[0, jnp.minimum(block + x, pairs - 1)].astype(jnp.float32)
+        padded[0:16, :] = jnp.where(block - 1 + x >= 0, low, 0.0)
         padded[16 : 16 + local_rows, :] = gathered[block].astype(jnp.float32)
-        padded[16 + local_rows : 32 + local_rows, :] = jnp.where(
-            block == pairs - 1, high_outer, high
-        )
+        padded[16 + local_rows : 32 + local_rows, :] = jnp.where(block + x < pairs, high, 0.0)
         windows = []
         for tap in range(KW):
             first = 16 + tap - KW // 2
             windows.append(padded[first : first + local_rows, :].astype(jnp.bfloat16))
         return dot(jnp.concatenate(windows, axis=1), wdec[...])
 
-    pass_weight(2)
-    pass_weight(3)
+    pass_weight(4)
     own_act.wait_recv()
     for core in range(2):
         for block in range(pairs):
-
-            @pl.when(jnp.logical_or(block != q, core != k))
-            def _():
-                remote(
-                    act.at[0, pl.ds(0, 16)],
-                    edges.at[core, block],
-                    edge_send.at[0],
-                    edge_recv.at[core, block],
-                    sibling,
-                ).wait_recv()
-
-    outside_copies[0].wait_recv()
-    pass_weight(4)
+            remote(
+                act.at[0, pl.ds(0, 16)],
+                edges.at[core, block],
+                edge_send.at[0],
+                edge_recv.at[core, block],
+                sibling,
+            ).wait_recv()
     for load in loads[7:]:
         load.wait()
     for copy in wf_copies:
         copy.wait_recv()
-    pass_act(1)
-    result = convolve(q)
+    pass_act(masks[0])
+    result = convolve(z)
     conv_copies = []
-    for step in range(1, pairs):
-        actf_copies[step].wait_recv()
-        if step + 1 < pairs:
-            pass_act(step + 1)
-        block = lax.rem(q - step + pairs, pairs)
-        conv_out[step - 1] = convolve(block).astype(jnp.bfloat16)
+    for step, mask in enumerate(masks):
+        actf_copies[mask].wait_recv()
+        if step + 1 < len(masks):
+            pass_act(masks[step + 1])
+        block = partner(mask)
+        conv_out[step] = convolve(block).astype(jnp.bfloat16)
         copy = remote(
-            conv_out.at[step - 1],
-            conv_in.at[step - 1],
-            conv_send.at[step],
-            conv_recv.at[step],
-            (g, h * pairs + block, k),
+            conv_out.at[step],
+            conv_in.at[step],
+            conv_send.at[mask],
+            conv_recv.at[mask],
+            (g, block * 2 + x, k),
         )
         copy.start()
         conv_copies.append(copy)
@@ -539,16 +509,11 @@
         + wf_copies
         + [part_copy, own_act, resid_copy]
         + edge_copies
-        + act_copies[1:]
-        + actf_copies[1:]
+        + list(act_copies.values())
+        + list(actf_copies.values())
         + conv_copies
     ):
         copy.wait_send()
-
-    @pl.when(meets)
-    def _():
-        for copy in outside_copies:
-            copy.wait_send()
 
 
 def fused_body(
@@ -593,7 +558,6 @@
         pltpu.VMEM((pairs, half, width), bf16),
         pltpu.VMEM((pairs, local_rows, width), bf16),
         pltpu.VMEM((2, pairs, 16, width), bf16),
-        pltpu.VMEM((16, width), bf16),
         pltpu.VMEM((local_rows + 32, width), f32),
         pltpu.VMEM((local_rows, out_half), bf16),
         pltpu.VMEM((2, half, out_half), bf16),
@@ -616,8 +580,6 @@
         dma((pairs,)),
         dma((2 * pairs,)),
         dma((2, pairs)),
-        dma((2 * pairs,)),
-        dma((1,)),
         dma((pairs,)),
         dma((pairs,)),
     ]

time: 43.5 us -> 36.5 us (0.84)
  Pallas kernels: 41.8 us -> 34.8 us
    pallas_call x1, Pallas kernels: 41.8 us -> 34.8 us  [fused_body(): pl.pallas_call(functools.partial(block_kernel, count), out_shape=jax.Shap...]
where the time goes in v3:
time: 36.5 us; the launch traced here: 36.3 us
  Pallas kernels  34.8 us (95%)
  local copies, waits for them, and re-layouts  1.54 us (4%)
    pallas_call x1, Pallas kernels, fused_body(): pl.pallas_call(functools.partial(block_kernel, count), out_shape=jax.Shap...  34.8 us
    unnamed x1, local copies, waits for them, and re-layouts  1.54 us

profile of v3, /device:TPU:0, one launch (start us, length us, event | category | flops | bytes accessed | tf_op | source)
XLA Modules:
  0.0 36.3 jit_solution(11745293165349875521)
XLA Ops:
  0.0 34.8 %shard_map.91 = bf16[128,384]{1,0:T(8,128)(2,1)} custom-call(bf16[1,128,1536]{2,1,0:T(8,128)(2,1)} %skip_hbm.1, f32[1536]{0:T(1024)} %attn_gain_hbm.1, bf16[1536,512]{1,0:T(8,128)(2,1)} %wq_hbm.1, bf16[1536,256]{1,0:T(8,128)(2,1)} %wkv_hbm.1, f32[1,4,4,32]{3,2,1,0:T(4,128)} %bias_hbm.1, bf16[512,1536]{1,0:T(8,128)(2,1)} %wout_hbm.1, f32[1536]{0:T(1024)} %dec_gain_hbm.1, ...), custom_call_target="tpu_custom_call" | custom-call | flops 754974720 | bytes 6000000 | tf_op jit(solution)/shard_map/pallas_call | solution.py:586
  34.8 1.5 %copy.11 = bf16[1,128,384]{2,1,0:T(8,128)(2,1)} copy(bf16[1,128,384]{2,1,0:T(8,128)(2,1)} %bitcast.1) | data formatting | bytes 196608

commit v4 on v3

--- a/solution.py
+++ b/solution.py
@@ -266,33 +266,7 @@
             barrier, inc=1, device_id=partner, device_id_type=pl.DeviceIdType.MESH
         )
 
-    loads[0].wait()
-    for load in loads[3:]:
-        load.start()
-    skip = skip_ref[0]
-    pooled = jnp.maximum(
-        dot(select_matrix(half, local_rows, lambda i, j: j == 2 * i), skip),
-        dot(select_matrix(half, local_rows, lambda i, j: j == 2 * i + 1), skip),
-    )
-    pooled_ref[...] = pooled
-    loads[1].wait()
-    normed = norm_scale(pooled, attn_gain_ref[...][None, :]).astype(jnp.bfloat16)
-    loads[2].wait()
-    kv[at(s * half, half, 16), :] = dot(normed, wkv[...]).astype(jnp.bfloat16)
-
     pl.semaphore_wait(barrier, len(partners))
-
-    def kv_rows(source, core):
-        return kv.at[at(source * half + core * quarter, quarter, 16)]
-
-    kv_copies = []
-    for step in range(1, count):
-        target = lax.rem(s + step, count)
-        copy = remote(
-            kv_rows(s, k), kv_rows(s, k), kv_send.at[step], kv_recv.at[step], (g, target, k)
-        )
-        copy.start()
-        kv_copies.append(copy)
 
     pair = s + 1 - 2 * x
     other_base = (1 - x) * own_depth
@@ -307,6 +281,33 @@
         )
         copy.start()
         w_copies.append(copy)
+
+    loads[0].wait()
+    for load in loads[3:]:
+        load.start()
+    skip = skip_ref[0]
+    pooled = jnp.maximum(
+        dot(select_matrix(half, local_rows, lambda i, j: j == 2 * i), skip),
+        dot(select_matrix(half, local_rows, lambda i, j: j == 2 * i + 1), skip),
+    )
+    pooled_ref[...] = pooled
+    loads[1].wait()
+    normed = norm_scale(pooled, attn_gain_ref[...][None, :]).astype(jnp.bfloat16)
+    loads[2].wait()
+    kv[at(s * half, half, 16), :] = dot(normed, wkv[...]).astype(jnp.bfloat16)
+
+    def kv_rows(source, core):
+        return kv.at[at(source * half + core * quarter, quarter, 16)]
+
+    kv_copies = []
+    for step in range(1, count):
+        target = lax.rem(s + step, count)
+        copy = remote(
+            kv_rows(s, k), kv_rows(s, k), kv_send.at[step], kv_recv.at[step], (g, target, k)
+        )
+        copy.start()
+        kv_copies.append(copy)
+
     wf_copies = []
 
     def pass_weight(tap):
@@ -375,7 +376,6 @@
     part_copy = remote(part_out, part_in, sib_send.at[0], sib_recv.at[0], sibling)
     part_copy.start()
     pass_weight(2)
-    pass_weight(3)
     part_copy.wait_recv()
     own = at(k * quarter, quarter, 16)
     attended = (
@@ -463,6 +463,7 @@
             windows.append(padded[first : first + local_rows, :].astype(jnp.bfloat16))
         return dot(jnp.concatenate(windows, axis=1), wdec[...])
 
+    pass_weight(3)
     pass_weight(4)
     own_act.wait_recv()
     for core in range(2):

time: 36.5 us -> 42.2 us (1.16)
  Pallas kernels: 34.8 us -> 40.5 us
    pallas_call x1, Pallas kernels: 34.8 us -> 40.5 us  [fused_body(): pl.pallas_call(functools.partial(block_kernel, count), out_shape=jax.Shap...]
where the time goes in v4:
time: 42.2 us; the launch traced here: 42 us
  Pallas kernels  40.5 us (96%)
  local copies, waits for them, and re-layouts  1.54 us (4%)
    pallas_call x1, Pallas kernels, fused_body(): pl.pallas_call(functools.partial(block_kernel, count), out_shape=jax.Shap...  40.5 us
    unnamed x1, local copies, waits for them, and re-layouts  1.54 us

profile of v4, /device:TPU:0, one launch (start us, length us, event | category | flops | bytes accessed | tf_op | source)
XLA Modules:
  0.0 42.0 jit_solution(3529104540114533700)
XLA Ops:
  0.0 40.5 %shard_map.91 = bf16[128,384]{1,0:T(8,128)(2,1)} custom-call(bf16[1,128,1536]{2,1,0:T(8,128)(2,1)} %skip_hbm.1, f32[1536]{0:T(1024)} %attn_gain_hbm.1, bf16[1536,512]{1,0:T(8,128)(2,1)} %wq_hbm.1, bf16[1536,256]{1,0:T(8,128)(2,1)} %wkv_hbm.1, f32[1,4,4,32]{3,2,1,0:T(4,128)} %bias_hbm.1, bf16[512,1536]{1,0:T(8,128)(2,1)} %wout_hbm.1, f32[1536]{0:T(1024)} %dec_gain_hbm.1, ...), custom_call_target="tpu_custom_call" | custom-call | flops 754974720 | bytes 6000000 | tf_op jit(solution)/shard_map/pallas_call | solution.py:587
  40.5 1.5 %copy.11 = bf16[1,128,384]{2,1,0:T(8,128)(2,1)} copy(bf16[1,128,384]{2,1,0:T(8,128)(2,1)} %bitcast.1) | data formatting | bytes 196608

commit v5 on v3

--- a/solution.py
+++ b/solution.py
@@ -297,7 +297,8 @@
     pair = s + 1 - 2 * x
     other_base = (1 - x) * own_depth
     w_copies = []
-    for tap in range(KW):
+
+    def send_weight(tap):
         copy = remote(
             wdec_hbm.at[tap, at(g * mid_depth, mid_depth, 16)],
             wdec.at[at(tap * width + x * own_depth + g * mid_depth, mid_depth, 16)],
@@ -307,6 +308,7 @@
         )
         copy.start()
         w_copies.append(copy)
+
     wf_copies = []
 
     def pass_weight(tap):
@@ -353,10 +355,10 @@
         )
         copy.start()
         kvf_copies.append(copy)
+    for tap in range(3):
+        send_weight(tap)
     for copy in kvf_copies:
         copy.wait_recv()
-    pass_weight(0)
-    pass_weight(1)
 
     scores = lax.dot_general(
         queries,
@@ -374,8 +376,10 @@
     part_out[...] = partial[at((1 - k) * quarter, quarter, 16), :].astype(jnp.bfloat16)
     part_copy = remote(part_out, part_in, sib_send.at[0], sib_recv.at[0], sibling)
     part_copy.start()
-    pass_weight(2)
-    pass_weight(3)
+    for tap in range(3, KW):
+        send_weight(tap)
+    pass_weight(0)
+    pass_weight(1)
     part_copy.wait_recv()
     own = at(k * quarter, quarter, 16)
     attended = (
@@ -463,7 +467,8 @@
             windows.append(padded[first : first + local_rows, :].astype(jnp.bfloat16))
         return dot(jnp.concatenate(windows, axis=1), wdec[...])
 
-    pass_weight(4)
+    for tap in range(2, KW):
+        pass_weight(tap)
     own_act.wait_recv()
     for core in range(2):
         for block in range(pairs):

time: 36.5 us -> 39 us (1.068)
  Pallas kernels: 34.8 us -> 37.3 us
    pallas_call x1, Pallas kernels: 34.8 us -> 37.3 us  [fused_body(): pl.pallas_call(functools.partial(block_kernel, count), out_shape=jax.Shap...]
where the time goes in v5:
time: 39 us; the launch traced here: 38.9 us
  Pallas kernels  37.3 us (96%)
  local copies, waits for them, and re-layouts  1.54 us (4%)
    pallas_call x1, Pallas kernels, fused_body(): pl.pallas_call(functools.partial(block_kernel, count), out_shape=jax.Shap...  37.3 us
    unnamed x1, local copies, waits for them, and re-layouts  1.54 us

profile of v5, /device:TPU:0, one launch (start us, length us, event | category | flops | bytes accessed | tf_op | source)
XLA Modules:
  0.0 38.9 jit_solution(13073450566635589535)
XLA Ops:
  0.0 37.3 %shard_map.91 = bf16[128,384]{1,0:T(8,128)(2,1)} custom-call(bf16[1,128,1536]{2,1,0:T(8,128)(2,1)} %skip_hbm.1, f32[1536]{0:T(1024)} %attn_gain_hbm.1, bf16[1536,512]{1,0:T(8,128)(2,1)} %wq_hbm.1, bf16[1536,256]{1,0:T(8,128)(2,1)} %wkv_hbm.1, f32[1,4,4,32]{3,2,1,0:T(4,128)} %bias_hbm.1, bf16[512,1536]{1,0:T(8,128)(2,1)} %wout_hbm.1, f32[1536]{0:T(1024)} %dec_gain_hbm.1, ...), custom_call_target="tpu_custom_call" | custom-call | flops 754974720 | bytes 6000000 | tf_op jit(solution)/shard_map/pallas_call | solution.py:591
  37.3 1.5 %copy.11 = bf16[1,128,384]{2,1,0:T(8,128)(2,1)} copy(bf16[1,128,384]{2,1,0:T(8,128)(2,1)} %bitcast.1) | data formatting | bytes 196608

commit v6 on v3

--- a/solution.py
+++ b/solution.py
@@ -451,7 +451,7 @@
         copy.start()
         actf_copies[step] = copy
 
-    def convolve(block):
+    def convolve(block, by_tap=False):
         low = edges[1, jnp.maximum(block - 1 + x, 0)].astype(jnp.float32)
         high = edges[0, jnp.minimum(block + x, pairs - 1)].astype(jnp.float32)
         padded[0:16, :] = jnp.where(block - 1 + x >= 0, low, 0.0)
@@ -461,7 +461,14 @@
         for tap in range(KW):
             first = 16 + tap - KW // 2
             windows.append(padded[first : first + local_rows, :].astype(jnp.bfloat16))
-        return dot(jnp.concatenate(windows, axis=1), wdec[...])
+        if not by_tap:
+            return dot(jnp.concatenate(windows, axis=1), wdec[...])
+        total = None
+        for tap in range(KW):
+            wf_copies[tap].wait_recv()
+            term = dot(windows[tap], wdec[tap * width : (tap + 1) * width])
+            total = term if total is None else total + term
+        return total
 
     pass_weight(4)
     own_act.wait_recv()
@@ -476,10 +483,8 @@
             ).wait_recv()
     for load in loads[7:]:
         load.wait()
-    for copy in wf_copies:
-        copy.wait_recv()
     pass_act(masks[0])
-    result = convolve(z)
+    result = convolve(z, by_tap=True)
     conv_copies = []
     for step, mask in enumerate(masks):
         actf_copies[mask].wait_recv()

time: 36.5 us -> 36.8 us (level)
  no operation moved by 1% of the time
where the time goes in v6:
time: 36.8 us; the launch traced here: 36.6 us
  Pallas kernels  35.1 us (95%)
  local copies, waits for them, and re-layouts  1.54 us (4%)
    pallas_call x1, Pallas kernels, fused_body(): pl.pallas_call(functools.partial(block_kernel, count), out_shape=jax.Shap...  35.1 us
    unnamed x1, local copies, waits for them, and re-layouts  1.54 us

profile of v6, /device:TPU:0, one launch (start us, length us, event | category | flops | bytes accessed | tf_op | source)
XLA Modules:
  0.0 36.6 jit_solution(4944580408245392637)
XLA Ops:
  0.0 35.1 %shard_map.91 = bf16[128,384]{1,0:T(8,128)(2,1)} custom-call(bf16[1,128,1536]{2,1,0:T(8,128)(2,1)} %skip_hbm.1, f32[1536]{0:T(1024)} %attn_gain_hbm.1, bf16[1536,512]{1,0:T(8,128)(2,1)} %wq_hbm.1, bf16[1536,256]{1,0:T(8,128)(2,1)} %wkv_hbm.1, f32[1,4,4,32]{3,2,1,0:T(4,128)} %bias_hbm.1, bf16[512,1536]{1,0:T(8,128)(2,1)} %wout_hbm.1, f32[1536]{0:T(1024)} %dec_gain_hbm.1, ...), custom_call_target="tpu_custom_call" | custom-call | flops 754974720 | bytes 6000000 | tf_op jit(solution)/shard_map/pallas_call | solution.py:591
  35.1 1.5 %copy.11 = bf16[1,128,384]{2,1,0:T(8,128)(2,1)} copy(bf16[1,128,384]{2,1,0:T(8,128)(2,1)} %bitcast.1) | data formatting | bytes 196608

commit v7 on v3

--- a/solution.py
+++ b/solution.py
@@ -297,7 +297,8 @@
     pair = s + 1 - 2 * x
     other_base = (1 - x) * own_depth
     w_copies = []
-    for tap in range(KW):
+
+    def send_weight(tap):
         copy = remote(
             wdec_hbm.at[tap, at(g * mid_depth, mid_depth, 16)],
             wdec.at[at(tap * width + x * own_depth + g * mid_depth, mid_depth, 16)],
@@ -307,6 +308,9 @@
         )
         copy.start()
         w_copies.append(copy)
+
+    for tap in range(3):
+        send_weight(tap)
     wf_copies = []
 
     def pass_weight(tap):
@@ -353,6 +357,8 @@
         )
         copy.start()
         kvf_copies.append(copy)
+    for tap in range(3, KW):
+        send_weight(tap)
     for copy in kvf_copies:
         copy.wait_recv()
     pass_weight(0)

time: 36.5 us -> 36.5 us (level)
  no operation moved by 1% of the time
where the time goes in v7:
time: 36.5 us; the launch traced here: 36.3 us
  Pallas kernels  34.8 us (95%)
  local copies, waits for them, and re-layouts  1.54 us (4%)
    pallas_call x1, Pallas kernels, fused_body(): pl.pallas_call(functools.partial(block_kernel, count), out_shape=jax.Shap...  34.8 us
    unnamed x1, local copies, waits for them, and re-layouts  1.54 us

profile of v7, /device:TPU:0, one launch (start us, length us, event | category | flops | bytes accessed | tf_op | source)
XLA Modules:
  0.0 36.3 jit_solution(13505419079117950819)
XLA Ops:
  0.0 34.8 %shard_map.91 = bf16[128,384]{1,0:T(8,128)(2,1)} custom-call(bf16[1,128,1536]{2,1,0:T(8,128)(2,1)} %skip_hbm.1, f32[1536]{0:T(1024)} %attn_gain_hbm.1, bf16[1536,512]{1,0:T(8,128)(2,1)} %wq_hbm.1, bf16[1536,256]{1,0:T(8,128)(2,1)} %wkv_hbm.1, f32[1,4,4,32]{3,2,1,0:T(4,128)} %bias_hbm.1, bf16[512,1536]{1,0:T(8,128)(2,1)} %wout_hbm.1, f32[1536]{0:T(1024)} %dec_gain_hbm.1, ...), custom_call_target="tpu_custom_call" | custom-call | flops 754974720 | bytes 6000000 | tf_op jit(solution)/shard_map/pallas_call | solution.py:592
  34.8 1.5 %copy.11 = bf16[1,128,384]{2,1,0:T(8,128)(2,1)} copy(bf16[1,128,384]{2,1,0:T(8,128)(2,1)} %bitcast.1) | data formatting | bytes 196608
